TPU v7x, 256 devices: a whole 4x4x8 slice. The times are simulated.
256 devices in a mesh: ctx: 32 (over x, y, core), tp: 8 (over z).
Axes of the slice: x: 4, y: 4, z: 8, core: 2. Of those that a mesh axis runs over, the one named last changes fastest.
Arguments:
- routed_x: bfloat16 [12288, 4096], P('ctx', 'tp'), may hold values from -20 to 20
- norm_gain: float32 [4096], replicated, may hold values from 0.1 to 1.9
- w_query: bfloat16 [4096, 4096], P(None, 'tp'), may hold values from -16 to 16
- w_key: bfloat16 [4096, 1024], P(None, 'tp'), may hold values from -1 to 1
- w_value: bfloat16 [4096, 1024], P(None, 'tp'), may hold values from -0.09375 to 0.09375
- w_out: bfloat16 [4096, 4096], P('tp'), may hold values from -0.5 to 0.5
- positions: int32 [12288], P('ctx'), may hold values from 0 to 262143, as said below
- counts: int32 [32], P('ctx'), may hold values from 96 to 384, as said below
- router_weight: float32 [12288], P('ctx'), may hold values from 0.25 to 1
Outputs:
- update: bfloat16 [12288, 4096], P('ctx', 'tp')
Inputs may be any that keep to these rules, and one draw needn't show every extreme that they name: Shard s's first counts[s] slots hold distinct increasing positions in [s * 8192, (s + 1) * 8192); its other slots hold 0. `counts`: each between 96 and 384; some shard has exactly 384.
All inputs are finite; a program needn't handle non-finite values.
Results may differ from a plain program's by a relative error of at most 0.02.
Values may be sent and summed in bfloat16 or wider, within the bound.
A program may use at most 128 MiB of HBM per device.

v0:
```python
import math

import jax
import jax.numpy as jnp
from jax import lax
from jax.sharding import PartitionSpec as P

HD = 128
TOK_DEV = 8192


def body(routed_x, norm_gain, w_query, w_key, w_value, w_out, positions, counts, router_weight):
    capacity = routed_x.shape[0]
    head_size = HD
    whole = lax.all_gather(routed_x, "tp", axis=1, tiled=True)
    widened = whole.astype(jnp.float32)
    normed = (
        widened * lax.rsqrt(jnp.mean(widened * widened, axis=-1, keepdims=True) + 1e-05) * norm_gain
    ).astype(jnp.bfloat16)
    queries = jnp.dot(normed, w_query, preferred_element_type=jnp.float32).astype(jnp.bfloat16)
    key_rows = jnp.dot(normed, w_key, preferred_element_type=jnp.float32).astype(jnp.bfloat16)
    value_rows = jnp.dot(normed, w_value, preferred_element_type=jnp.float32).astype(jnp.bfloat16)
    kv_heads = w_key.shape[1] // head_size
    group_size = w_query.shape[1] // w_key.shape[1]
    total_tokens = TOK_DEV * lax.axis_size("ctx")
    is_live = jnp.arange(capacity, dtype=jnp.int32) < counts[0]
    query_pos = jnp.where(is_live, positions, total_tokens)
    key_pos = jnp.where(is_live, positions, total_tokens + 1)
    query_heads = queries.reshape(capacity, kv_heads, group_size, head_size)
    scale = head_size ** (-0.5)
    start_state = (
        jnp.full((kv_heads, group_size, capacity), -1e30, jnp.float32),
        jnp.zeros((kv_heads, group_size, capacity), jnp.float32),
        jnp.zeros((kv_heads, group_size, capacity, head_size), jnp.float32),
    )

    def absorb(carry_state, key_block, value_block, pos_block):
        running_max, totals, numerator = carry_state
        key_count = key_block.shape[0]
        key_heads = key_block.reshape(key_count, kv_heads, head_size)
        value_heads = value_block.reshape(key_count, kv_heads, head_size)
        scores = (
            jnp.einsum("qkgd,nkd->kgqn", query_heads, key_heads, preferred_element_type=jnp.float32)
            * scale
        )
        allowed = pos_block[None, None, None, :] <= query_pos[None, None, :, None]
        masked = jnp.where(allowed, scores, -1e30)
        new_max = jnp.maximum(running_max, jnp.max(masked, axis=-1))
        weights = jnp.where(allowed, jnp.exp(masked - new_max[..., None]), 0.0)
        factor = jnp.exp(running_max - new_max)
        totals = totals * factor + jnp.sum(weights, axis=-1)
        numerator = numerator * factor[..., None] + jnp.einsum(
            "kgqn,nkd->kgqd",
            weights.astype(jnp.bfloat16),
            value_heads,
            preferred_element_type=jnp.float32,
        )
        return (new_max, totals, numerator)

    key_block = lax.all_gather(key_rows, "ctx", axis=0, tiled=True)
    value_block = lax.all_gather(value_rows, "ctx", axis=0, tiled=True)
    pos_block = lax.all_gather(key_pos, "ctx", axis=0, tiled=True)
    key_count = key_block.shape[0]
    block_rows = math.gcd(key_count, 2048)
    blocks = key_count // block_rows
    stacked = (
        key_block.reshape(blocks, block_rows, key_block.shape[1]),
        value_block.reshape(blocks, block_rows, value_block.shape[1]),
        pos_block.reshape(blocks, block_rows),
    )

    def scan_step(inner, block_item):
        return (absorb(inner, block_item[0], block_item[1], block_item[2]), None)

    result, unused = lax.scan(scan_step, start_state, stacked)
    running_max, totals, numerator = result
    heads_out = (numerator / totals[..., None]).astype(jnp.bfloat16)
    heads_out = heads_out.transpose(2, 0, 1, 3).reshape(capacity, kv_heads * group_size * head_size)
    partial_term = jnp.dot(heads_out, w_out, preferred_element_type=jnp.float32).astype(
        jnp.bfloat16
    )
    partial_term = lax.optimization_barrier(partial_term).astype(jnp.float32)
    summed = lax.psum_scatter(
        partial_term.astype(jnp.bfloat16), "tp", scatter_dimension=1, tiled=True
    ).astype(jnp.float32)
    update = jnp.where(is_live[:, None], router_weight[:, None] * summed, 0.0)
    return update.astype(jnp.bfloat16)


def solution(mesh):
    return jax.shard_map(
        body,
        mesh=mesh,
        in_specs=(
            P("ctx", "tp"),
            P(),
            P(None, "tp"),
            P(None, "tp"),
            P(None, "tp"),
            P("tp", None),
            P("ctx"),
            P("ctx"),
            P("ctx"),
        ),
        out_specs=P("ctx", "tp"),
        check_vma=False,
    )
```

profile of v0, /device:TPU:4, one launch (start us, length us, event | category | flops | bytes accessed | tf_op | source)
XLA Modules:
  0.0 346.4 jit_solution(442035128994070212)
XLA Ops:
  6.5 0.7 all-gather.5.cloned.1.call-update
  7.3 0.0 all-gather.7.cloned.1.call-start
  7.3 49.8 %all-gather.5.cloned.1.call-done = bf16[384,4096]{1,0:T(8,128)(2,1)} async-done(((bf16[384,512]{1,0:T(8,128)(2,1)}), bf16[384,4096]{1,0:T(8,128)(2,1)}) %all-gather.5.cloned.1.call-update) | async-done | bytes 3145744 | tf_op jit(solution)/shard_map/all_gather | solution.py:15
  57.1 2.6 fusion.25
  59.7 3.6 %convolution_convert_fusion.3 = bf16[384,128]{1,0:T(8,128)(2,1)} fusion(bf16[4096,128]{1,0:T(8,128)(2,1)S(1)} %copy-done, bf16[384,4096]{1,0:T(8,128)(2,1)} %all-gather.5.cloned.1.call-done, f32[4096]{0:T(1024)} %param.12, f32[384]{0:T(512)S(1)} %add_rsqrt_fusion), kind=kOutput, calls=%fused_computation.37 | convolution fusion | flops 408993792 | bytes 4310528 | tf_op jit(solution)/shard_map/dot_general | solution.py:21
  63.3 0.0 all-gather.7.cloned.1.call-update
  63.3 0.0 all-gather.9.cloned.1.call-start
  63.4 3.6 %convolution_convert_fusion.2 = bf16[384,128]{1,0:T(8,128)(2,1)} fusion(bf16[4096,128]{1,0:T(8,128)(2,1)S(1)} %copy-done.4, bf16[384,4096]{1,0:T(8,128)(2,1)} %all-gather.5.cloned.1.call-done, f32[4096]{0:T(1024)S(1)} %copy-done.5, f32[384]{0:T(512)S(1)} %add_rsqrt_fusion), kind=kOutput, calls=%fused_computation.36 | convolution fusion | flops 408993792 | bytes 4310528 | tf_op jit(solution)/shard_map/dot_general | solution.py:22
  66.9 0.0 all-gather.9.cloned.1.call-update
  66.9 0.0 reduce-scatter.2.cloned.1.call-start
  67.7 22.8 %all-gather = s32[32,1,384]{2,1,0:T(1,128)S(1)} all-gather(s32[1,1,384]{2,1,0:T(1,128)S(1)} %reshape.104), channel_id=1, replica_groups=mesh['ctx'=32,'tp'=8] {'ctx'}, dimensions={0}, use_global_device_ids=true | all-gather | bytes 50688 | tf_op jit(solution)/shard_map/all_gather | solution.py:62
  90.5 0.1 reduce.2
  90.7 5.0 %convolution_convert_fusion.1 = bf16[384,512]{1,0:T(8,128)(2,1)S(1)} fusion(bf16[4096,512]{1,0:T(8,128)(2,1)} %param.13, bf16[384,4096]{1,0:T(8,128)(2,1)} %all-gather.5.cloned.1.call-done, f32[4096]{0:T(1024)S(1)} %copy-done.5, f32[384]{0:T(512)S(1)} %add_rsqrt_fusion), kind=kOutput, calls=%fused_computation.35 | convolution fusion | flops 1617100800 | bytes 7751168 | tf_op jit(solution)/shard_map/dot_general | solution.py:20
  95.7 0.1 reshape.101
  95.8 0.1 copy.16
  95.8 15.6 %all-gather.7.cloned.1.call-done = bf16[12288,128]{1,0:T(8,128)(2,1)} async-done(((bf16[384,128]{1,0:T(8,128)(2,1)}), bf16[12288,128]{1,0:T(8,128)(2,1)}) %all-gather.7.cloned.1.call-update) | async-done | bytes 3145744 | tf_op jit(solution)/shard_map/all_gather | solution.py:60
  111.4 52.1 %all-gather.9.cloned.1.call-done = bf16[12288,128]{1,0:T(8,128)(2,1)} async-done(((bf16[384,128]{1,0:T(8,128)(2,1)}), bf16[12288,128]{1,0:T(8,128)(2,1)}) %all-gather.9.cloned.1.call-update) | async-done | bytes 3145744 | tf_op jit(solution)/shard_map/all_gather | solution.py:61
  163.5 121.4 %while.15 = (s32[]{:T(128)}, f32[1,4,384]{2,1,0:T(4,128)S(1)}, f32[1,4,384]{2,1,0:T(4,128)S(1)}, f32[1,4,384,128]{3,2,1,0:T(8,128)S(1)}, s32[6,2048]{1,0:T(8,128...) while((s32[]{:T(128)}, f32[1,4,384]{2,1,0:T(4,128)S(1)}, ...), condition=%wide.region_4.5_spmd.clone, body=%wide.region_1.4_spmd.clone.sunk | while | flops 1652892672 | bytes 94366360 | solution.py:75
  163.5 0.6 broadcast_compare_fusion.2
  164.1 7.8 %fusion.44 = (f32[4,384]{1,0:T(4,128)S(1)}, f32[2048,384,4]{1,0,2:T(8,128)}) fusion(pred[384,2048]{0,1:T(8,128)(4,1)S(1)} %broadcast_compare_fusion.2, bf16[384,1,4,128]{3,0,2,1:T(8,128)(2,1)S(1)} %get-tuple-element.228, bf16[6,2048,128]{2,1,0:T(8,128)(2,1)} %get-tuple-element.227, s32[]{:T(128)} %get-tuple-element.210), kind=kOutput, calls=%fused_computation.2.clone.1 | convolution fusion | flops 814742016 | bytes 14293504 | tf_op jit(solution)/shard_map/while/body/eval_jaxpr/qkgd,nkd->kgqn/dot_general | solution.py:43
  171.9 8.6 %fusion.47 = f32[1,4,384,128]{3,2,1,0:T(8,128)S(1)} fusion(f32[2048,384,4]{1,0,2:T(8,128)} %get-tuple-element.197, f32[4,384]{1,0:T(4,128)S(1)} %bitcast.92, pred[384,2048]{0,1:T(8,128)(4,1)S(1)} %broadcast_compare_fusion.2, f32[1,4,384,128]{3,2,1,0:T(8,128)S(1)} %get-tuple-element.213, bf16[6,2048,128]{2,1,0:T(8,128)(2,1)} %get-tuple-element.229, ...), kind=kOutput, calls=%fused_computation.10.clone.1 | convolution fusion | flops 821624832 | bytes 15479297 | tf_op jit(solution)/shard_map/while/body/eval_jaxpr/kgqn,nkd->kgqd/dot_general | solution.py:52
  180.6 3.2 fusion.46
  183.8 0.6 broadcast_compare_fusion.2
  184.4 7.8 %fusion.44 = (f32[4,384]{1,0:T(4,128)S(1)}, f32[2048,384,4]{1,0,2:T(8,128)}) fusion(pred[384,2048]{0,1:T(8,128)(4,1)S(1)} %broadcast_compare_fusion.2, bf16[384,1,4,128]{3,0,2,1:T(8,128)(2,1)S(1)} %get-tuple-element.228, bf16[6,2048,128]{2,1,0:T(8,128)(2,1)} %get-tuple-element.227, s32[]{:T(128)} %get-tuple-element.210), kind=kOutput, calls=%fused_computation.2.clone.1 | convolution fusion | flops 814742016 | bytes 14293504 | tf_op jit(solution)/shard_map/while/body/eval_jaxpr/qkgd,nkd->kgqn/dot_general | solution.py:43
  192.2 8.6 %fusion.47 = f32[1,4,384,128]{3,2,1,0:T(8,128)S(1)} fusion(f32[2048,384,4]{1,0,2:T(8,128)} %get-tuple-element.197, f32[4,384]{1,0:T(4,128)S(1)} %bitcast.92, pred[384,2048]{0,1:T(8,128)(4,1)S(1)} %broadcast_compare_fusion.2, f32[1,4,384,128]{3,2,1,0:T(8,128)S(1)} %get-tuple-element.213, bf16[6,2048,128]{2,1,0:T(8,128)(2,1)} %get-tuple-element.229, ...), kind=kOutput, calls=%fused_computation.10.clone.1 | convolution fusion | flops 821624832 | bytes 15479297 | tf_op jit(solution)/shard_map/while/body/eval_jaxpr/kgqn,nkd->kgqd/dot_general | solution.py:52
  200.8 3.2 fusion.46
  204.0 0.6 broadcast_compare_fusion.2
  204.6 7.8 %fusion.44 = (f32[4,384]{1,0:T(4,128)S(1)}, f32[2048,384,4]{1,0,2:T(8,128)}) fusion(pred[384,2048]{0,1:T(8,128)(4,1)S(1)} %broadcast_compare_fusion.2, bf16[384,1,4,128]{3,0,2,1:T(8,128)(2,1)S(1)} %get-tuple-element.228, bf16[6,2048,128]{2,1,0:T(8,128)(2,1)} %get-tuple-element.227, s32[]{:T(128)} %get-tuple-element.210), kind=kOutput, calls=%fused_computation.2.clone.1 | convolution fusion | flops 814742016 | bytes 14293504 | tf_op jit(solution)/shard_map/while/body/eval_jaxpr/qkgd,nkd->kgqn/dot_general | solution.py:43
  212.4 8.6 %fusion.47 = f32[1,4,384,128]{3,2,1,0:T(8,128)S(1)} fusion(f32[2048,384,4]{1,0,2:T(8,128)} %get-tuple-element.197, f32[4,384]{1,0:T(4,128)S(1)} %bitcast.92, pred[384,2048]{0,1:T(8,128)(4,1)S(1)} %broadcast_compare_fusion.2, f32[1,4,384,128]{3,2,1,0:T(8,128)S(1)} %get-tuple-element.213, bf16[6,2048,128]{2,1,0:T(8,128)(2,1)} %get-tuple-element.229, ...), kind=kOutput, calls=%fused_computation.10.clone.1 | convolution fusion | flops 821624832 | bytes 15479297 | tf_op jit(solution)/shard_map/while/body/eval_jaxpr/kgqn,nkd->kgqd/dot_general | solution.py:52
  221.0 3.2 fusion.46
  224.3 0.6 broadcast_compare_fusion.2
  224.9 7.8 %fusion.44 = (f32[4,384]{1,0:T(4,128)S(1)}, f32[2048,384,4]{1,0,2:T(8,128)}) fusion(pred[384,2048]{0,1:T(8,128)(4,1)S(1)} %broadcast_compare_fusion.2, bf16[384,1,4,128]{3,0,2,1:T(8,128)(2,1)S(1)} %get-tuple-element.228, bf16[6,2048,128]{2,1,0:T(8,128)(2,1)} %get-tuple-element.227, s32[]{:T(128)} %get-tuple-element.210), kind=kOutput, calls=%fused_computation.2.clone.1 | convolution fusion | flops 814742016 | bytes 14293504 | tf_op jit(solution)/shard_map/while/body/eval_jaxpr/qkgd,nkd->kgqn/dot_general | solution.py:43
  232.7 8.6 %fusion.47 = f32[1,4,384,128]{3,2,1,0:T(8,128)S(1)} fusion(f32[2048,384,4]{1,0,2:T(8,128)} %get-tuple-element.197, f32[4,384]{1,0:T(4,128)S(1)} %bitcast.92, pred[384,2048]{0,1:T(8,128)(4,1)S(1)} %broadcast_compare_fusion.2, f32[1,4,384,128]{3,2,1,0:T(8,128)S(1)} %get-tuple-element.213, bf16[6,2048,128]{2,1,0:T(8,128)(2,1)} %get-tuple-element.229, ...), kind=kOutput, calls=%fused_computation.10.clone.1 | convolution fusion | flops 821624832 | bytes 15479297 | tf_op jit(solution)/shard_map/while/body/eval_jaxpr/kgqn,nkd->kgqd/dot_general | solution.py:52
  241.3 3.2 fusion.46
  244.5 0.6 broadcast_compare_fusion.2
  245.1 7.8 %fusion.44 = (f32[4,384]{1,0:T(4,128)S(1)}, f32[2048,384,4]{1,0,2:T(8,128)}) fusion(pred[384,2048]{0,1:T(8,128)(4,1)S(1)} %broadcast_compare_fusion.2, bf16[384,1,4,128]{3,0,2,1:T(8,128)(2,1)S(1)} %get-tuple-element.228, bf16[6,2048,128]{2,1,0:T(8,128)(2,1)} %get-tuple-element.227, s32[]{:T(128)} %get-tuple-element.210), kind=kOutput, calls=%fused_computation.2.clone.1 | convolution fusion | flops 814742016 | bytes 14293504 | tf_op jit(solution)/shard_map/while/body/eval_jaxpr/qkgd,nkd->kgqn/dot_general | solution.py:43
  252.9 8.6 %fusion.47 = f32[1,4,384,128]{3,2,1,0:T(8,128)S(1)} fusion(f32[2048,384,4]{1,0,2:T(8,128)} %get-tuple-element.197, f32[4,384]{1,0:T(4,128)S(1)} %bitcast.92, pred[384,2048]{0,1:T(8,128)(4,1)S(1)} %broadcast_compare_fusion.2, f32[1,4,384,128]{3,2,1,0:T(8,128)S(1)} %get-tuple-element.213, bf16[6,2048,128]{2,1,0:T(8,128)(2,1)} %get-tuple-element.229, ...), kind=kOutput, calls=%fused_computation.10.clone.1 | convolution fusion | flops 821624832 | bytes 15479297 | tf_op jit(solution)/shard_map/while/body/eval_jaxpr/kgqn,nkd->kgqd/dot_general | solution.py:52
  261.5 3.2 fusion.46
  264.8 0.6 broadcast_compare_fusion.2
  265.4 7.8 %fusion.44 = (f32[4,384]{1,0:T(4,128)S(1)}, f32[2048,384,4]{1,0,2:T(8,128)}) fusion(pred[384,2048]{0,1:T(8,128)(4,1)S(1)} %broadcast_compare_fusion.2, bf16[384,1,4,128]{3,0,2,1:T(8,128)(2,1)S(1)} %get-tuple-element.228, bf16[6,2048,128]{2,1,0:T(8,128)(2,1)} %get-tuple-element.227, s32[]{:T(128)} %get-tuple-element.210), kind=kOutput, calls=%fused_computation.2.clone.1 | convolution fusion | flops 814742016 | bytes 14293504 | tf_op jit(solution)/shard_map/while/body/eval_jaxpr/qkgd,nkd->kgqn/dot_general | solution.py:43
  273.2 8.6 %fusion.47 = f32[1,4,384,128]{3,2,1,0:T(8,128)S(1)} fusion(f32[2048,384,4]{1,0,2:T(8,128)} %get-tuple-element.197, f32[4,384]{1,0:T(4,128)S(1)} %bitcast.92, pred[384,2048]{0,1:T(8,128)(4,1)S(1)} %broadcast_compare_fusion.2, f32[1,4,384,128]{3,2,1,0:T(8,128)S(1)} %get-tuple-element.213, bf16[6,2048,128]{2,1,0:T(8,128)(2,1)} %get-tuple-element.229, ...), kind=kOutput, calls=%fused_computation.10.clone.1 | convolution fusion | flops 821624832 | bytes 15479297 | tf_op jit(solution)/shard_map/while/body/eval_jaxpr/kgqn,nkd->kgqd/dot_general | solution.py:52
  281.8 3.2 fusion.46
  285.0 0.3 copy.17
  285.3 0.1 divide_convert_fusion
  285.3 5.7 %convolution_convert_fusion = bf16[384,4096]{1,0:T(8,128)(2,1)} fusion(bf16[384,512]{0,1:T(8,128)(2,1)S(1)} %bitcast.94, bf16[512,4096]{1,0:T(8,128)(2,1)} %param.16), kind=kOutput, calls=%fused_computation.34 | convolution fusion | flops 1612185600 | bytes 7733248 | tf_op jit(solution)/shard_map/dot_general | solution.py:79
  291.0 0.0 reduce-scatter.2.cloned.1.call-update
  291.0 46.9 %reduce-scatter.2.cloned.1.call-done = bf16[384,512]{1,0:T(8,128)(2,1)} async-done(((bf16[384,4096]{1,0:T(8,128)(2,1)}), bf16[384,512]{1,0:T(8,128)(2,1)}) %reduce-scatter.2.cloned.1.call-update) | async-done | bytes 393232 | tf_op jit(solution)/shard_map/reduce_scatter | solution.py:83
  338.0 1.9 select_convert_fusion
  (55 shorter events, 0.4 us)
Async XLA Ops:
  6.5 53.2 %copy-start = (bf16[4096,128]{1,0:T(8,128)(2,1)S(1)}, bf16[4096,128]{1,0:T(8,128)(2,1)}, u32[]{:S(2)}) copy-start(bf16[4096,128]{1,0:T(8,128)(2,1)} %param.14) | copy-start | bytes 3145732
  6.5 50.6 %all-gather.5.cloned.1.call-start = ((), (), s32[]{:S(2)}) async-start(), calls=%async_computation.1 | async-start | bytes 3538944 | tf_op jit(solution)/shard_map/all_gather | solution.py:15
  7.3 56.1 %copy-start.4 = (bf16[4096,128]{1,0:T(8,128)(2,1)S(1)}, bf16[4096,128]{1,0:T(8,128)(2,1)}, u32[]{:S(2)}) copy-start(bf16[4096,128]{1,0:T(8,128)(2,1)} %param.15) | copy-start | bytes 3145732
  7.3 56.1 %copy-start.5 = (f32[4096]{0:T(1024)S(1)}, f32[4096]{0:T(1024)}, u32[]{:S(2)}) copy-start(f32[4096]{0:T(1024)} %param.12) | copy-start | bytes 49156
  7.3 104.1 %all-gather.7.cloned.1.call-start = ((), (), s32[]{:S(2)}) async-start(), calls=%async_computation.2 | async-start | bytes 3244032 | tf_op jit(solution)/shard_map/all_gather | solution.py:60
  63.3 4.4 %copy-start.3 = (s32[384]{0:T(512)S(1)}, s32[384]{0:T(512)}, u32[]{:S(2)}) copy-start(s32[384]{0:T(512)} %param.17) | copy-start | bytes 4612
  63.3 100.2 %all-gather.9.cloned.1.call-start = ((), (), s32[]{:S(2)}) async-start(), calls=%async_computation.3 | async-start | bytes 3244032 | tf_op jit(solution)/shard_map/all_gather | solution.py:61
  66.9 271.1 %reduce-scatter.2.cloned.1.call-start = ((), (), s32[]{:S(2)}) async-start(), calls=%async_computation.4 | async-start | bytes 3538944 | tf_op jit(solution)/shard_map/reduce_scatter | solution.py:83
  171.9 8.6 %copy-start.1 = (f32[2048,384,4]{1,0,2:T(8,128)S(1)}, f32[2048,384,4]{1,0,2:T(8,128)}, u32[]{:S(2)}) copy-start(f32[2048,384,4]{1,0,2:T(8,128)} %get-tuple-element.197) | copy-start | bytes 37748740 | tf_op jit(solution)/shard_map/while
  192.2 8.6 %copy-start.1 = (f32[2048,384,4]{1,0,2:T(8,128)S(1)}, f32[2048,384,4]{1,0,2:T(8,128)}, u32[]{:S(2)}) copy-start(f32[2048,384,4]{1,0,2:T(8,128)} %get-tuple-element.197) | copy-start | bytes 37748740 | tf_op jit(solution)/shard_map/while
  212.4 8.6 %copy-start.1 = (f32[2048,384,4]{1,0,2:T(8,128)S(1)}, f32[2048,384,4]{1,0,2:T(8,128)}, u32[]{:S(2)}) copy-start(f32[2048,384,4]{1,0,2:T(8,128)} %get-tuple-element.197) | copy-start | bytes 37748740 | tf_op jit(solution)/shard_map/while
  232.7 8.6 %copy-start.1 = (f32[2048,384,4]{1,0,2:T(8,128)S(1)}, f32[2048,384,4]{1,0,2:T(8,128)}, u32[]{:S(2)}) copy-start(f32[2048,384,4]{1,0,2:T(8,128)} %get-tuple-element.197) | copy-start | bytes 37748740 | tf_op jit(solution)/shard_map/while
  252.9 8.6 %copy-start.1 = (f32[2048,384,4]{1,0,2:T(8,128)S(1)}, f32[2048,384,4]{1,0,2:T(8,128)}, u32[]{:S(2)}) copy-start(f32[2048,384,4]{1,0,2:T(8,128)} %get-tuple-element.197) | copy-start | bytes 37748740 | tf_op jit(solution)/shard_map/while
  273.1 8.6 %copy-start.1 = (f32[2048,384,4]{1,0,2:T(8,128)S(1)}, f32[2048,384,4]{1,0,2:T(8,128)}, u32[]{:S(2)}) copy-start(f32[2048,384,4]{1,0,2:T(8,128)} %get-tuple-element.197) | copy-start | bytes 37748740 | tf_op jit(solution)/shard_map/while
  285.3 52.7 %copy-start.2 = (f32[384]{0:T(512)S(1)}, f32[384]{0:T(512)}, u32[]{:S(2)}) copy-start(f32[384]{0:T(512)} %param.19) | copy-start | bytes 4612
Sparse Core Ops, SparseCore 0:
  9.2 47.9 all-gather.4
  63.4 47.9 all-gather.6
  114.0 49.5 all-gather.8
  291.2 46.7 reduce-scatter.1
where the time goes:
time: 347 us; the launch traced here: 346 us
  waiting for transfers between devices  165 us (48%)
  matrix products  116 us (33%)
  other arithmetic  27.4 us (8%)
  blocking collectives  22.8 us (7%)
  between operations  13.9 us (4%)
    all_gather x1, waiting for transfers between devices, body(): value_block = lax.all_gather(value_rows, 'ctx', axis=0, tiled=True)  52.1 us
    dot_general x6, matrix products, absorb(): jnp.einsum('kgqn,nkd->kgqd', weights.astype(jnp.bfloat16), value_heads, p...  51.6 us
    all_gather x1, waiting for transfers between devices, body(): whole = lax.all_gather(routed_x, 'tp', axis=1, tiled=True)  49.8 us
    reduce_scatter x1, waiting for transfers between devices, body(): lax.psum_scatter(partial_term.astype(jnp.bfloat16), 'tp', scatter_dimensi...  46.9 us
    dot_general x6, matrix products, absorb(): jnp.einsum('qkgd,nkd->kgqn', query_heads, key_heads, preferred_element_ty...  46.6 us
    all_gather x1, blocking collectives, body(): pos_block = lax.all_gather(key_pos, 'ctx', axis=0, tiled=True)  22.8 us
    reduce_sum x6, other arithmetic, absorb(): totals = totals * factor + jnp.sum(weights, axis=-1)  18.9 us
    all_gather x1, waiting for transfers between devices, body(): key_block = lax.all_gather(key_rows, 'ctx', axis=0, tiled=True)  15.6 us
  transfers between devices with their start and end apart: 4, of which 4 were waited for; matrix products, arithmetic and copies ran while one was open for 3% of the time, Pallas kernels for 0%

commit v1 on v0

v1 whole, which is shorter than its diff:
```python
import jax
import jax.numpy as jnp
from jax import lax
from jax.experimental import pallas as pl
from jax.experimental.pallas import tpu as pltpu
from jax.sharding import PartitionSpec as P

HD = 128
GROUP = 4
ROWS = 384
CHUNK = 128
CHUNKS = 3
FEATURES = 512
Q_ROWS = GROUP * CHUNK
K_TILE = HD + 16
NX, NY, NZ = 4, 4, 8
NEG = -1e30
LOG2E = 1.4426950408889634
BF16 = jnp.bfloat16
F32 = jnp.float32

SCHEDULE = (
    ["zs00", "zs10", "own", "z01", "zs20", "z02", "z11", "z03", "z12", "z04", "fin0", "kva0"]
    + ["z13", "kvb0", "z21", "kvc0", "z14", "fin1", "kva1", "kvd0", "z22", "kvb1", "kve0"]
    + ["z23", "kvc1", "kvf0", "kvd1", "at00", "z24", "fin2", "kva2", "kve1", "kvf1"]
    + ["at01", "kvb2", "at10", "kvc2", "at11", "kvd2", "at20", "kve2", "at21", "kvf2"]
    + ["at02", "ho0", "rs01", "at12", "ho1", "rs02", "rs11", "at22", "ho2", "rs03", "rs12", "rs21"]
    + ["rs04", "rs13", "rs22", "rs05", "rs14", "rs23", "rs15", "rs24", "rs25"]
)


def dot(a, b):
    return jnp.dot(a, b, preferred_element_type=F32)


def kernel(
    x_ref, gain_ref, wq_hbm, wk_hbm, wv_hbm, wo_hbm, count_ref, router_ref, out_ref,
    xg, wq, wkv, wo, acc_q, acc_kv, ssq, qs, kt, va, m_s, l_s, o_s, ho, sb, rb,
    w_sem, z_send, z_recv, kv_send, kv_recv, sib_send, sib_recv, rs_send, rs_recv,
):
    ctx = lax.axis_index("ctx")
    t = lax.axis_index("tp")
    core = lax.rem(ctx, 2)
    y = lax.rem(lax.div(ctx, 2), NY)
    x = lax.div(ctx, 2 * NY)

    def at(xx, yy, cc, tt):
        return ((lax.rem(xx, NX) * NY + lax.rem(yy, NY)) * 2 + cc, lax.rem(tt, NZ))

    z_next = (at(x, y, core, t + 1), at(x, y, core, t + NZ - 1))
    x_next = (at(x + 1, y, core, t), at(x + NX - 1, y, core, t))
    y_next = (at(x, y + 1, core, t), at(x, y + NY - 1, core, t))
    sibling = at(x, y, 1 - core, t)
    count = count_ref[0]

    weights = [
        pltpu.make_async_copy(wq_hbm, wq, w_sem.at[0]),
        pltpu.make_async_copy(wk_hbm, wkv.at[:, pl.ds(0, HD)], w_sem.at[1]),
        pltpu.make_async_copy(wv_hbm, wkv.at[:, pl.ds(HD, HD)], w_sem.at[2]),
        pltpu.make_async_copy(wo_hbm, wo, w_sem.at[3]),
    ]
    for copy in weights:
        copy.start()

    barrier = pltpu.get_barrier_semaphore()
    peers = z_next + x_next + y_next + (sibling,)
    for peer in peers:
        pl.semaphore_signal(barrier, inc=1, device_id=peer, device_id_type=pl.DeviceIdType.MESH)
    pl.semaphore_wait(barrier, len(peers))

    sends = []

    def remote(src, dst, send_sem, recv_sem, device):
        return pltpu.make_async_remote_copy(
            src_ref=src, dst_ref=dst, send_sem=send_sem, recv_sem=recv_sem,
            device_id=device, device_id_type=pl.DeviceIdType.MESH,
        )

    def send(src, dst, send_sem, recv_sem, device):
        copy = remote(src, dst, send_sem, recv_sem, device)
        copy.start()
        sends.append(copy)

    def arrived(dst, send_sem, recv_sem, device):
        remote(dst, dst, send_sem, recv_sem, device).wait_recv()

    def z_rows(d, k, h):
        if h < 4:
            return pl.ds(k * CHUNK, CHUNK)
        return pl.ds(k * CHUNK + d * (CHUNK // 2), CHUNK // 2)

    def z_start(k, h):
        for d, sign in enumerate((1, -1)):
            block = lax.rem(t - sign * (h - 1) + NZ, NZ)
            dst = xg.at[block, z_rows(d, k, h)]
            src = x_ref.at[z_rows(d, k, h)] if h == 1 else dst
            send(src, dst, z_send.at[d, k, h - 1], z_recv.at[d, k, h - 1], z_next[d])

    def project(block, values, rows):
        widened = values.astype(F32)
        squares = widened * widened
        ssq[rows] += sum(squares[:, i * 128 : (i + 1) * 128] for i in range(FEATURES // 128))
        scaled = (widened * gain_ref[block]).astype(BF16)
        features = pl.ds(pl.multiple_of(block * FEATURES, FEATURES), FEATURES)
        acc_q[rows] += dot(scaled, wq[features])
        acc_kv[rows] += dot(scaled, wkv[features])

    def z_step(k, h):
        for d, sign in enumerate((1, -1)):
            block = lax.rem(t - sign * h + NZ, NZ)
            arrived(
                xg.at[block, z_rows(d, k, h)], z_send.at[d, k, h - 1], z_recv.at[d, k, h - 1], z_next[d]
            )
        if h < 4:
            z_start(k, h + 1)
        rows = pl.ds(k * CHUNK, CHUNK)
        for sign in (1, -1) if h < 4 else (1,):
            block = lax.rem(t - sign * h + NZ, NZ)
            project(block, xg[block, rows], rows)

    def own():
        for copy in weights[:3]:
            copy.wait()
        ssq[...] = jnp.zeros_like(ssq)
        acc_q[...] = jnp.zeros_like(acc_q)
        acc_kv[...] = jnp.zeros_like(acc_kv)
        m_s[...] = jnp.full_like(m_s, NEG)
        l_s[...] = jnp.zeros_like(l_s)
        o_s[...] = jnp.zeros_like(o_s)
        project(t, x_ref[...], pl.ds(0, ROWS))

    def finish(k):
        rows = pl.ds(k * CHUNK, CHUNK)
        mean = jnp.sum(ssq[rows], axis=1, keepdims=True) * (1.0 / (NZ * FEATURES))
        inverse = lax.rsqrt(mean + 1e-05)
        query = (acc_q[rows] * (inverse * (HD**-0.5 * LOG2E))).astype(BF16)
        for h in range(GROUP):
            qs[k, h * CHUNK : (h + 1) * CHUNK, :] = query[:, h * HD : (h + 1) * HD]
        pair = acc_kv[rows] * inverse
        kt[k, core, y, x, 0:HD, :] = jnp.transpose(pair[:, :HD]).astype(BF16)
        slot = lax.broadcasted_iota(jnp.int32, (16, CHUNK), 1) + k * CHUNK
        kt[k, core, y, x, HD:K_TILE, :] = jnp.where(slot < count, 0.0, NEG).astype(BF16)
        va[k, core, x, y, :, :] = pair[:, HD:].astype(BF16)

    kinds = (
        (kt, x, y, x_next, y_next, ((0, 80), (80, 64))),
        (va, y, x, y_next, x_next, ((0, 64), (64, 64))),
    )

    def kv_sems(k, a, phase, d, hop):
        return kv_send.at[k, a, phase, d, hop], kv_recv.at[k, a, phase, d, hop]

    def kva(k):
        for a, (buf, inner, outer, inner_next, outer_next, parts) in enumerate(kinds):
            tile = buf.at[k, core, outer, inner]
            for d in range(2):
                send(tile, tile, *kv_sems(k, a, 0, d, 0), inner_next[d])

    def kvb(k):
        for a, (buf, inner, outer, inner_next, outer_next, parts) in enumerate(kinds):
            for d in range(2):
                source = lax.rem(inner + (3, 1)[d], 4)
                tile = buf.at[k, core, outer, source]
                arrived(tile, *kv_sems(k, a, 0, d, 0), inner_next[d])
                part = buf.at[k, core, outer, source, pl.ds(*parts[d])]
                send(part, part, *kv_sems(k, a, 0, d, 1), inner_next[d])

    def kvc(k):
        for a, (buf, inner, outer, inner_next, outer_next, parts) in enumerate(kinds):
            for d in range(2):
                source = lax.rem(inner + 2, 4)
                part = buf.at[k, core, outer, source, pl.ds(*parts[d])]
                arrived(part, *kv_sems(k, a, 0, d, 1), inner_next[d])
            line = buf.at[k, core, outer]
            for d in range(2):
                send(line, line, *kv_sems(k, a, 1, d, 0), outer_next[d])
            send(line, line, sib_send.at[k, a, 0], sib_recv.at[k, a, 0], sibling)

    def kvd(k):
        for a, (buf, inner, outer, inner_next, outer_next, parts) in enumerate(kinds):
            for d in range(2):
                source = lax.rem(outer + (3, 1)[d], 4)
                line = buf.at[k, core, source]
                arrived(line, *kv_sems(k, a, 1, d, 0), outer_next[d])
                part = buf.at[k, core, source, pl.ds(2 * d, 2)]
                send(part, part, *kv_sems(k, a, 1, d, 1), outer_next[d])
                send(line, line, sib_send.at[k, a, 1 + d], sib_recv.at[k, a, 1 + d], sibling)

    def kve(k):
        for a, (buf, inner, outer, inner_next, outer_next, parts) in enumerate(kinds):
            source = lax.rem(outer + 2, 4)
            for d in range(2):
                part = buf.at[k, core, source, pl.ds(2 * d, 2)]
                arrived(part, *kv_sems(k, a, 1, d, 1), outer_next[d])
            line = buf.at[k, core, source]
            send(line, line, sib_send.at[k, a, 3], sib_recv.at[k, a, 3], sibling)

    def kvf(k):
        for a, (buf, inner, outer, inner_next, outer_next, parts) in enumerate(kinds):
            for i, shift in enumerate((0, 3, 1, 2)):
                line = buf.at[k, 1 - core, lax.rem(outer + shift, 4)]
                arrived(line, sib_send.at[k, a, i], sib_recv.at[k, a, i], sibling)

    def absorb(r, j, g, edge):
        keys, bias, values = [], [], []
        xx = lax.div(g, 2)
        place = lax.rem(ctx, 4)
        for i in range(4):
            yy = lax.rem(g, 2) * 2 + i // 2
            keys.append(kt[j, i % 2, yy, xx, 0:HD, :])
            row = kt[j, i % 2, yy, xx, HD:K_TILE, :].astype(F32)[0:1, :]
            if edge and j != r:
                seen = i <= place if j < r else i < place
                row = row + jnp.where(seen, 0.0, NEG)
            bias.append(row)
            values.append(va[j, i % 2, xx, yy, :, :])
        scores = dot(qs[r], jnp.concatenate(keys, axis=1)) + jnp.concatenate(bias, axis=1)
        if edge and j == r:
            slot = lax.rem(lax.broadcasted_iota(jnp.int32, (Q_ROWS, CHUNK), 0), CHUNK)
            key = lax.broadcasted_iota(jnp.int32, (Q_ROWS, CHUNK), 1)
            ahead = key - slot
            pieces = []
            for i in range(4):
                limit = jnp.where(i < place, CHUNK, jnp.where(i == place, 0, -CHUNK))
                pieces.append(
                    jnp.where(ahead <= limit, scores[:, i * CHUNK : (i + 1) * CHUNK], NEG)
                )
            scores = jnp.concatenate(pieces, axis=1)
        before = m_s[r]
        after = jnp.maximum(before, jnp.max(scores, axis=1, keepdims=True))
        factor = jnp.exp2(before - after)
        probs = jnp.exp2(scores - jnp.concatenate([after] * 4, axis=1))
        m_s[r] = after
        l_s[r] = l_s[r] * factor + sum(probs[:, i * CHUNK : (i + 1) * CHUNK] for i in range(4))
        o_s[r] = o_s[r] * factor + dot(probs.astype(BF16), jnp.concatenate(values, axis=0))

    def attend(r, j):
        lax.fori_loop(0, lax.div(ctx, 4), lambda g, c: (absorb(r, j, g, False), c)[1], 0)
        absorb(r, j, lax.div(ctx, 4), True)

    def heads(r):
        if r == 0:
            weights[3].wait()
        mixed = (o_s[r] / jnp.sum(l_s[r], axis=1, keepdims=True)).astype(BF16)
        for h in range(GROUP):
            ho[r, :, h * HD : (h + 1) * HD] = mixed[h * CHUNK : (h + 1) * CHUNK, :]

    def term(r, block):
        block = lax.rem(block + NZ, NZ)
        columns = pl.ds(pl.multiple_of(block * FEATURES, FEATURES), FEATURES)
        return dot(ho[r], wo[:, columns])

    half = CHUNK // 2

    def rs(r, step):
        def rs_sems(d, hop):
            return rs_send.at[d, r, hop], rs_recv.at[d, r, hop]

        def rows(d, hop):
            return pl.ds(d * half, half) if hop == 0 else pl.ds(0, CHUNK)

        if step == 1:
            product = term(r, t + 4).astype(BF16)
            for d in range(2):
                sb[d, r, 0, rows(d, 0)] = product[d * half : (d + 1) * half]
        elif step < 5:
            for d, sign in enumerate((1, -1)):
                product = term(r, t + sign * (5 - step))
                landed = rb.at[d, r, step - 2, rows(d, step - 2)]
                arrived(landed, *rs_sems(d, step - 2), z_next[d])
                if step == 2:
                    keep = product[(1 - d) * half : (2 - d) * half].astype(BF16)
                    sb[d, r, 1, rows(1 - d, 0)] = keep
                    add = product[d * half : (d + 1) * half] + landed[...].astype(F32)
                    sb[d, r, 1, rows(d, 0)] = add.astype(BF16)
                else:
                    sb[d, r, step - 1] = (product + landed[...].astype(F32)).astype(BF16)
        if step < 5:
            for d in range(2):
                src = sb.at[d, r, step - 1, rows(d, step - 1)]
                dst = rb.at[d, r, step - 1, rows(d, step - 1)]
                send(src, dst, *rs_sems(d, step - 1), z_next[d])
            return
        total = term(r, t)
        for d in range(2):
            landed = rb.at[d, r, 3]
            arrived(landed, *rs_sems(d, 3), z_next[d])
            total = total + landed[...].astype(F32)
        weight = jnp.transpose(jnp.broadcast_to(router_ref[r : r + 1, :], (CHUNK, CHUNK)))
        total = total * jnp.concatenate([weight] * 4, axis=1)
        slot = lax.broadcasted_iota(jnp.int32, (CHUNK, FEATURES), 0) + r * CHUNK
        out_ref[pl.ds(r * CHUNK, CHUNK)] = jnp.where(slot < count, total, 0.0).astype(BF16)

    steps = {"kva": kva, "kvb": kvb, "kvc": kvc, "kvd": kvd, "kve": kve, "kvf": kvf}
    for event in SCHEDULE:
        if event == "own":
            own()
        elif event[:2] == "zs":
            z_start(int(event[2]), int(event[3]) + 1)
        elif event[0] == "z":
            z_step(int(event[1]), int(event[2]))
        elif event[:3] == "fin":
            finish(int(event[3]))
        elif event[:2] == "kv":
            steps[event[:3]](int(event[3]))
        elif event[:2] == "at":
            attend(int(event[2]), int(event[3]))
        elif event[:2] == "ho":
            heads(int(event[2]))
        else:
            rs(int(event[2]), int(event[3]))
    for copy in sends:
        copy.wait_send()


def body(routed_x, norm_gain, w_query, w_key, w_value, w_out, positions, counts, router_weight):
    vmem = pl.BlockSpec(memory_space=pltpu.VMEM)
    hbm = pl.BlockSpec(memory_space=pl.ANY)
    smem = pl.BlockSpec(memory_space=pltpu.SMEM)
    return pl.pallas_call(
        kernel,
        out_shape=jax.ShapeDtypeStruct((ROWS, FEATURES), BF16),
        in_specs=[vmem, vmem, hbm, hbm, hbm, hbm, smem, vmem],
        out_specs=vmem,
        scratch_shapes=[
            pltpu.VMEM((NZ, ROWS, FEATURES), BF16),
            pltpu.VMEM((NZ * FEATURES, GROUP * HD), BF16),
            pltpu.VMEM((NZ * FEATURES, 2 * HD), BF16),
            pltpu.VMEM((GROUP * HD, NZ * FEATURES), BF16),
            pltpu.VMEM((ROWS, GROUP * HD), F32),
            pltpu.VMEM((ROWS, 2 * HD), F32),
            pltpu.VMEM((ROWS, 128), F32),
            pltpu.VMEM((CHUNKS, Q_ROWS, HD), BF16),
            pltpu.VMEM((CHUNKS, 2, NY, NX, K_TILE, CHUNK), BF16),
            pltpu.VMEM((CHUNKS, 2, NX, NY, CHUNK, HD), BF16),
            pltpu.VMEM((CHUNKS, Q_ROWS, 128), F32),
            pltpu.VMEM((CHUNKS, Q_ROWS, 128), F32),
            pltpu.VMEM((CHUNKS, Q_ROWS, HD), F32),
            pltpu.VMEM((CHUNKS, CHUNK, GROUP * HD), BF16),
            pltpu.VMEM((2, CHUNKS, 4, CHUNK, FEATURES), BF16),
            pltpu.VMEM((2, CHUNKS, 4, CHUNK, FEATURES), BF16),
            pltpu.SemaphoreType.DMA((4,)),
            pltpu.SemaphoreType.DMA((2, CHUNKS, 4)),
            pltpu.SemaphoreType.DMA((2, CHUNKS, 4)),
            pltpu.SemaphoreType.DMA((CHUNKS, 2, 2, 2, 2)),
            pltpu.SemaphoreType.DMA((CHUNKS, 2, 2, 2, 2)),
            pltpu.SemaphoreType.DMA((CHUNKS, 2, 4)),
            pltpu.SemaphoreType.DMA((CHUNKS, 2, 4)),
            pltpu.SemaphoreType.DMA((2, CHUNKS, 4)),
            pltpu.SemaphoreType.DMA((2, CHUNKS, 4)),
        ],
        compiler_params=pltpu.CompilerParams(
            collective_id=0, has_side_effects=True, vmem_limit_bytes=56 * 1024 * 1024
        ),
    )(
        routed_x,
        norm_gain.reshape(NZ, 1, FEATURES),
        w_query,
        w_key,
        w_value,
        w_out,
        counts,
        router_weight.reshape(CHUNKS, CHUNK),
    )


def solution(mesh):
    return jax.shard_map(
        body,
        mesh=mesh,
        in_specs=(
            P("ctx", "tp"),
            P(),
            P(None, "tp"),
            P(None, "tp"),
            P(None, "tp"),
            P("tp", None),
            P("ctx"),
            P("ctx"),
            P("ctx"),
        ),
        out_specs=P("ctx", "tp"),
        check_vma=False,
    )
```

time: 347 us -> 131 us (0.38)
  the two profiles are of different devices: /device:TPU:4 before, /device:TPU:22 now
where the time goes in v1:
time: 131 us
  Pallas kernels  128 us (98%)
  local copies, waits for them, and re-layouts  1.77 us (1%)
    pallas_call x1, Pallas kernels, body(): pl.pallas_call(kernel, out_shape=jax.ShapeDtypeStruct((ROWS, FEATURES), B...  128 us

profile of v1, /device:TPU:22, one launch (start us, length us, event | category | flops | bytes accessed | tf_op | source)
XLA Modules:
  0.0 130.8 jit_solution(16337512438065822734)
XLA Ops:
  0.7 128.4 %shard_map.82 = bf16[384,512]{1,0:T(8,128)(2,1)} custom-call(bf16[384,512]{1,0:T(8,128)(2,1)} %x_ref.1, f32[8,1,512]{2,1,0:T(1,128)} %bitcast.2, bf16[4096,512]{1,0:T(8,128)(2,1)} %wq_hbm.1, bf16[4096,128]{1,0:T(8,128)(2,1)} %wk_hbm.1, bf16[4096,128]{1,0:T(8,128)(2,1)} %wv_hbm.1, bf16[512,4096]{1,0:T(8,128)(2,1)} %wo_hbm.1, s32[1]{0:T(128)S(6)} %copy.10.count_ref, ...), custom_call_target="tpu_custom_call" | custom-call | tf_op jit(solution)/shard_map/pallas_call | solution.py:320
  129.1 1.8 %copy.11 = bf16[384,512]{1,0:T(8,128)(2,1)} copy(bf16[384,512]{1,0:T(8,128)(2,1)} %shard_map.82) | data formatting | bytes 786432

commit v2 on v1

v2 whole, which is shorter than its diff:
```python
import jax
import jax.numpy as jnp
from jax import lax
from jax.experimental import pallas as pl
from jax.experimental.pallas import tpu as pltpu
from jax.sharding import PartitionSpec as P

HD = 128
GROUP = 4
ROWS = 384
CHUNK = 128
CHUNKS = 3
FEATURES = 512
Q_ROWS = GROUP * CHUNK
SHARDS = 8
K_TILE = HD + 16
NX, NY, NZ = 4, 4, 8
NEG = -1e30
LOG2E = 1.4426950408889634
BF16 = jnp.bfloat16
F32 = jnp.float32

PIECES = ((0, 128, 0), (128, 64, 1), (192, 64, 1))
PIECES += ((256, 32, 2), (288, 32, 2), (320, 32, 2), (352, 32, 2))
SCHEDULE = (
    "zs0 zs1 zs2 own", "z01 pj01 z11 z21", "pj11 z02 pj02 z12", "z22 pj12 z03 pj03",
    "z13 zs3 z23 pj13", "zs4 zs5 zs6 z04", "pj04 fin0 kva0 fq0", "z14 z31 z24 pj14",
    "fin1 kva1 fq1 z41", "z51 z61 pj21 z32", "z42 kvb0 z52 z62", "pj22 z33 kvb1 z43",
    "z53 z63 pj23 z34", "z44 z54 z64 pk24", "fin2 kva2 pq24 fq2", "gq kvc0 kvd0 at00",
    "kvb2 kvc1 gw al1", "kvd1 ap1 kvc2 al2", "kvd2 at32 gs at02", "ho0 rs01 tma0 at12",
    "rs02 ho1 rs11 tma1", "tmb0 at22 gr ho2", "rs21 tma2 rs12 rs03", "tmb1 rs22 rs13 rs04",
    "tmb2 rs23 rs14 rs05", "rs24 rs15 rs25",
)


def dot(a, b):
    return jnp.dot(a, b, preferred_element_type=F32)


def kernel(
    x_hbm, gain_hbm, wq_hbm, wk_hbm, wv_hbm, wo_hbm, count_ref, router_hbm, out_hbm,
    xg, gain_ref, router_ref, out_ref, wq, wkv, wo, acc_q, acc_kv, ssq, qs, kt, va, m_s, l_s, o_s, ho, tm, sb, rb,
    w_sem, z_send, z_recv, kv_send, kv_recv, sib_send, sib_recv, rs_send, rs_recv,
    guest_sem, out_sem,
):
    ctx = lax.axis_index("ctx")
    t = lax.axis_index("tp")
    core = lax.rem(ctx, 2)
    y = lax.rem(lax.div(ctx, 2), NY)
    x = lax.div(ctx, 2 * NY)

    def at(xx, yy, cc, tt):
        return ((lax.rem(xx, NX) * NY + lax.rem(yy, NY)) * 2 + cc, lax.rem(tt, NZ))

    z_next = (at(x, y, core, t + 1), at(x, y, core, t + NZ - 1))
    x_line = tuple(at(x + i, y, core, t) for i in (1, 3, 2))
    y_line = tuple(at(x, y + i, core, t) for i in (1, 3, 2))
    sibling = at(x, y, 1 - core, t)
    count = count_ref[0]

    weights = [
        pltpu.make_async_copy(wq_hbm, wq, w_sem.at[0]),
        pltpu.make_async_copy(wk_hbm, wkv.at[:, pl.ds(0, HD)], w_sem.at[1]),
        pltpu.make_async_copy(wv_hbm, wkv.at[:, pl.ds(HD, HD)], w_sem.at[2]),
        pltpu.make_async_copy(gain_hbm, gain_ref, w_sem.at[3]),
        pltpu.make_async_copy(x_hbm, xg.at[t], w_sem.at[4]),
        pltpu.make_async_copy(wo_hbm, wo, w_sem.at[5]),
        pltpu.make_async_copy(router_hbm, router_ref, w_sem.at[6]),
    ]
    for copy in weights:
        copy.start()

    barrier = pltpu.get_barrier_semaphore()
    peers = z_next + x_line + y_line + (sibling,)
    for peer in peers:
        pl.semaphore_signal(barrier, inc=1, device_id=peer, device_id_type=pl.DeviceIdType.MESH)
    pl.semaphore_wait(barrier, len(peers))

    sends = []

    def remote(src, dst, send_sem, recv_sem, device):
        return pltpu.make_async_remote_copy(
            src_ref=src, dst_ref=dst, send_sem=send_sem, recv_sem=recv_sem,
            device_id=device, device_id_type=pl.DeviceIdType.MESH,
        )

    def send(src, dst, send_sem, recv_sem, device):
        copy = remote(src, dst, send_sem, recv_sem, device)
        copy.start()
        sends.append(copy)

    def arrived(dst, send_sem, recv_sem, device):
        remote(dst, dst, send_sem, recv_sem, device).wait_recv()

    def z_rows(d, p, h):
        first, size, chunk = PIECES[p]
        if h < 4:
            return pl.ds(first, size)
        return pl.ds(first + d * (size // 2), size // 2)

    def z_start(p, h):
        for d, sign in enumerate((1, -1)):
            block = lax.rem(t - sign * (h - 1) + NZ, NZ)
            dst = xg.at[block, z_rows(d, p, h)]
            src = x_hbm.at[z_rows(d, p, h)] if h == 1 else dst
            send(src, dst, z_send.at[d, p, h - 1], z_recv.at[d, p, h - 1], z_next[d])

    def project(block, rows, keys, queries):
        widened = xg[block, rows].astype(F32)
        scaled = (widened * gain_ref[block]).astype(BF16)
        features = pl.ds(pl.multiple_of(block * FEATURES, FEATURES), FEATURES)
        if keys:
            squares = widened * widened
            ssq[rows] += sum(squares[:, i * 128 : (i + 1) * 128] for i in range(FEATURES // 128))
            acc_kv[rows] += dot(scaled, wkv[features])
        if queries:
            acc_q[rows] += dot(scaled, wq[features])

    def z_step(p, h):
        for d, sign in enumerate((1, -1)):
            block = lax.rem(t - sign * h + NZ, NZ)
            arrived(
                xg.at[block, z_rows(d, p, h)], z_send.at[d, p, h - 1], z_recv.at[d, p, h - 1], z_next[d]
            )
        if h < 4:
            z_start(p, h + 1)

    def z_project(k, h, keys=True, queries=True):
        for sign in (1, -1) if h < 4 else (1,):
            block = lax.rem(t - sign * h + NZ, NZ)
            project(block, pl.ds(k * CHUNK, CHUNK), keys, queries)

    def own():
        for copy in weights[:5]:
            copy.wait()
        ssq[...] = jnp.zeros_like(ssq)
        acc_q[...] = jnp.zeros_like(acc_q)
        acc_kv[...] = jnp.zeros_like(acc_kv)
        m_s[...] = jnp.full_like(m_s, NEG)
        l_s[...] = jnp.zeros_like(l_s)
        o_s[...] = jnp.zeros_like(o_s)
        project(t, pl.ds(0, ROWS), True, True)

    def row_scale(rows):
        mean = jnp.sum(ssq[rows], axis=1, keepdims=True) * (1.0 / (NZ * FEATURES))
        return lax.rsqrt(mean + 1e-05)

    def finish_queries(k):
        rows = pl.ds(k * CHUNK, CHUNK)
        query = (acc_q[rows] * (row_scale(rows) * (HD**-0.5 * LOG2E))).astype(BF16)
        for h in range(GROUP):
            qs[k, h * CHUNK : (h + 1) * CHUNK, :] = query[:, h * HD : (h + 1) * HD]

    def finish_keys(k):
        rows = pl.ds(k * CHUNK, CHUNK)
        pair = acc_kv[rows] * row_scale(rows)
        kt[k, core, y, x, 0:HD, :] = jnp.transpose(pair[:, :HD]).astype(BF16)
        slot = lax.broadcasted_iota(jnp.int32, (16, CHUNK), 1) + k * CHUNK
        kt[k, core, y, x, HD:K_TILE, :] = jnp.where(slot < count, 0.0, NEG).astype(BF16)
        va[k, core, x, y, :, :] = pair[:, HD:].astype(BF16)

    kinds = ((kt, x, y, x_line, y_line), (va, y, x, y_line, x_line))

    def kv_sems(k, a, phase, i):
        return kv_send.at[k, a, phase, i], kv_recv.at[k, a, phase, i]

    def kva(k):
        for a, (buf, inner, outer, inner_line, outer_line) in enumerate(kinds):
            tile = buf.at[k, core, outer, inner]
            for i in range(3):
                send(tile, tile, *kv_sems(k, a, 0, i), inner_line[i])

    def kvb(k):
        for a, (buf, inner, outer, inner_line, outer_line) in enumerate(kinds):
            for i in range(3):
                tile = buf.at[k, core, outer, lax.rem(inner + (3, 1, 2)[i], 4)]
                arrived(tile, *kv_sems(k, a, 0, i), inner_line[i])
            line = buf.at[k, core, outer]
            for i in range(3):
                send(line, line, *kv_sems(k, a, 1, i), outer_line[i])
            send(line, line, sib_send.at[k, a, 3], sib_recv.at[k, a, 3], sibling)

    def kvc(k):
        for i in range(3):
            for a, (buf, inner, outer, inner_line, outer_line) in enumerate(kinds):
                line = buf.at[k, core, lax.rem(outer + (3, 1, 2)[i], 4)]
                arrived(line, *kv_sems(k, a, 1, i), outer_line[i])
                send(line, line, sib_send.at[k, a, i], sib_recv.at[k, a, i], sibling)

    def kvd(k):
        for a, (buf, inner, outer, inner_line, outer_line) in enumerate(kinds):
            for i in range(4):
                line = buf.at[k, 1 - core, lax.rem(outer + (3, 1, 2, 0)[i], 4)]
                arrived(line, sib_send.at[k, a, i], sib_recv.at[k, a, i], sibling)

    place = lax.rem(ctx, SHARDS)
    host, lender = x == 0, x == NX - 1

    def absorb(r, chunk, j, g, last, pair=False):
        count_rows = 2 * Q_ROWS if pair else Q_ROWS
        slot = lax.rem(lax.broadcasted_iota(jnp.int32, (count_rows, CHUNK), 0), CHUNK)
        if pair:
            half_rows = lax.broadcasted_iota(jnp.int32, (count_rows, CHUNK), 0)
            slot = jnp.where(half_rows < Q_ROWS, slot, slot + CHUNK)
        slot = slot.astype(F32)

        def rows_of(ref):
            return ref[0:2].reshape(count_rows, HD) if pair else ref[r]

        def put(ref, value):
            if pair:
                ref[0:2] = value.reshape(2, Q_ROWS, HD)
            else:
                ref[r] = value

        column = lax.broadcasted_iota(jnp.int32, (1, CHUNK), 1)
        keys, first, values = [], [], []
        own_limit = jnp.where(j < chunk, CHUNK, jnp.where(j == chunk, 0, -CHUNK))
        if pair:
            own_limit = -j * CHUNK
        for i in range(SHARDS):
            keys.append(kt[j, i % 2, i // 2, g, 0:HD, :])
            mask = kt[j, i % 2, i // 2, g, HD:K_TILE, :].astype(F32)[0:1, :]
            limit = jnp.where(i < place, ROWS, jnp.where(i == place, own_limit, -ROWS))
            limit = jnp.where(g < last, ROWS, limit)
            first.append(jnp.where(mask < 0.0, 1e9, (column - limit).astype(F32)))
            values.append(va[j, i % 2, g, i // 2, :, :])
        scores = dot(rows_of(qs), jnp.concatenate(keys, axis=1))
        scores = [
            jnp.where(first[i] <= slot, scores[:, i * CHUNK : (i + 1) * CHUNK], NEG)
            for i in range(SHARDS)
        ]
        scores = jnp.concatenate(scores, axis=1)
        before = rows_of(m_s)
        after = jnp.maximum(before, jnp.max(scores, axis=1, keepdims=True))
        factor = jnp.exp2(before - after)
        probs = jnp.exp2(scores - jnp.concatenate([after] * SHARDS, axis=1))
        put(m_s, after)
        lanes = sum(probs[:, i * CHUNK : (i + 1) * CHUNK] for i in range(SHARDS))
        put(l_s, rows_of(l_s) * factor + lanes)
        mixed = dot(probs.astype(BF16), jnp.concatenate(values, axis=0))
        put(o_s, rows_of(o_s) * factor + mixed)

    def attend(r, j):
        guest = jnp.int32(r) == 3
        lent = (jnp.int32(r) == 2) & lender
        last = jnp.where(guest, NX - 1, x)
        groups = jnp.where(guest, jnp.where(host, NX, 0), jnp.where(lent, 0, x + 1))
        chunk = jnp.minimum(jnp.int32(r), 2)

        @pl.loop(0, groups)
        def _(g):
            absorb(r, chunk, jnp.int32(j), g, last)

    def attend_pair(j):
        pl.loop(0, x + 1)(lambda g: absorb(0, 0, jnp.int32(j), g, x, pair=True))

    def attend_many(first):
        if first == 1:
            pl.loop(1, 4)(lambda r: attend(r, 0))
        else:
            pl.loop(2, 4)(lambda r: attend(r, 1))

    def guest_copy(back):
        i = 1 if back else 0
        src = ho.at[3] if back else qs.at[2]
        dst = ho.at[2] if back else qs.at[3]
        return remote(src, dst, guest_sem.at[i], guest_sem.at[2 + i], x_line[i])

    def guest_query():
        pl.when(lender)(lambda: guest_copy(False).start())

    def guest_wait():
        pl.when(host)(lambda: guest_copy(False).wait_recv())

    def guest_send():
        @pl.when(host)
        def _():
            mix(3)
            guest_copy(True).start()

    def guest_return():
        pl.when(lender)(lambda: guest_copy(True).wait_recv())

    def mix(r):
        mixed = (o_s[r] / jnp.sum(l_s[r], axis=1, keepdims=True)).astype(BF16)
        for h in range(GROUP):
            ho[r, :, h * HD : (h + 1) * HD] = mixed[h * CHUNK : (h + 1) * CHUNK, :]

    def heads(r):
        if r == 0:
            weights[5].wait()
            weights[6].wait()
        if r == 2:
            pl.when(jnp.logical_not(lender))(lambda: mix(2))
        else:
            mix(r)

    def term(r, block):
        block = lax.rem(block + NZ, NZ)
        columns = pl.ds(pl.multiple_of(block * FEATURES, FEATURES), FEATURES)
        return dot(ho[r], wo[:, columns])

    half = CHUNK // 2

    def result_copy(r):
        return pltpu.make_async_copy(
            out_ref.at[r], out_hbm.at[pl.ds(r * CHUNK, CHUNK)], out_sem.at[r]
        )

    def terms(r, shifts):
        for shift in shifts:
            tm[r, shift + 3] = term(r, t + shift)

    def rs(r, step):
        def rs_sems(d, hop):
            return rs_send.at[d, r, hop], rs_recv.at[d, r, hop]

        def rows(d, hop):
            return pl.ds(d * half, half) if hop == 0 else pl.ds(0, CHUNK)

        if step == 1:
            product = term(r, t + 4).astype(BF16)
            for d in range(2):
                sb[d, r, 0, rows(d, 0)] = product[d * half : (d + 1) * half]
        for d, sign in enumerate((1, -1)):
            if step == 5:
                break
            if step > 1:
                product = tm.at[r, 3 + sign * (5 - step)]
                landed = rb.at[d, r, step - 2, rows(d, step - 2)]
                arrived(landed, *rs_sems(d, step - 2), z_next[d])
                if step == 2:
                    sb[d, r, 1, rows(1 - d, 0)] = product[rows(1 - d, 0)].astype(BF16)
                add = product[rows(d, step - 2)] + landed[...].astype(F32)
                sb[d, r, step - 1, rows(d, step - 2)] = add.astype(BF16)
            src = sb.at[d, r, step - 1, rows(d, step - 1)]
            dst = rb.at[d, r, step - 1, rows(d, step - 1)]
            send(src, dst, *rs_sems(d, step - 1), z_next[d])
        if step < 5:
            return
        total = tm[r, 3]
        for d in range(2):
            landed = rb.at[d, r, 3]
            arrived(landed, *rs_sems(d, 3), z_next[d])
            total = total + landed[...].astype(F32)
        weight = jnp.transpose(jnp.broadcast_to(router_ref[r : r + 1, :], (CHUNK, CHUNK)))
        total = total * jnp.concatenate([weight] * 4, axis=1)
        slot = lax.broadcasted_iota(jnp.int32, (CHUNK, FEATURES), 0) + r * CHUNK
        out_ref[r] = jnp.where(slot < count, total, 0.0).astype(BF16)
        result_copy(r).start()

    steps = {"zs": lambda p: z_start(p, 1), "z": z_step, "pj": z_project}
    steps |= {"pk": lambda k, h: z_project(k, h, queries=False), "fin": finish_keys}
    steps |= {"pq": lambda k, h: z_project(k, h, keys=False), "fq": finish_queries}
    steps |= {"kva": kva, "kvb": kvb, "kvc": kvc, "kvd": kvd}
    steps |= {"gq": guest_query, "gw": guest_wait, "gs": guest_send, "gr": guest_return}
    steps |= {"al": attend_many, "ap": attend_pair, "own": own, "at": attend, "ho": heads, "tma": lambda r: terms(r, (3, -3)), "tmb": lambda r: terms(r, (2, -2, 1, -1, 0)), "rs": rs}
    for event in " ".join(SCHEDULE).split():
        name = event.rstrip("0123456789")
        steps[name](*map(int, event[len(name) :]))
    for copy in sends:
        copy.wait_send()
    for r in range(CHUNKS):
        result_copy(r).wait()
    pl.when(lender)(lambda: guest_copy(False).wait_send())
    pl.when(host)(lambda: guest_copy(True).wait_send())


def body(routed_x, norm_gain, w_query, w_key, w_value, w_out, positions, counts, router_weight):
    hbm = pl.BlockSpec(memory_space=pl.ANY)
    smem = pl.BlockSpec(memory_space=pltpu.SMEM)
    return pl.pallas_call(
        kernel,
        out_shape=jax.ShapeDtypeStruct((ROWS, FEATURES), BF16),
        in_specs=[hbm] * 6 + [smem, hbm],
        out_specs=hbm,
        scratch_shapes=[
            pltpu.VMEM((NZ, ROWS, FEATURES), BF16),
            pltpu.VMEM((NZ, 1, FEATURES), F32),
            pltpu.VMEM((CHUNKS, CHUNK), F32),
            pltpu.VMEM((CHUNKS, CHUNK, FEATURES), BF16),
            pltpu.VMEM((NZ * FEATURES, GROUP * HD), BF16),
            pltpu.VMEM((NZ * FEATURES, 2 * HD), BF16),
            pltpu.VMEM((GROUP * HD, NZ * FEATURES), BF16),
            pltpu.VMEM((ROWS, GROUP * HD), F32),
            pltpu.VMEM((ROWS, 2 * HD), F32),
            pltpu.VMEM((ROWS, 128), F32),
            pltpu.VMEM((CHUNKS + 1, Q_ROWS, HD), BF16),
            pltpu.VMEM((CHUNKS, 2, NY, NX, K_TILE, CHUNK), BF16),
            pltpu.VMEM((CHUNKS, 2, NX, NY, CHUNK, HD), BF16),
            pltpu.VMEM((CHUNKS + 1, Q_ROWS, 128), F32),
            pltpu.VMEM((CHUNKS + 1, Q_ROWS, 128), F32),
            pltpu.VMEM((CHUNKS + 1, Q_ROWS, HD), F32),
            pltpu.VMEM((CHUNKS + 1, CHUNK, GROUP * HD), BF16),
            pltpu.VMEM((CHUNKS, 7, CHUNK, FEATURES), F32),
            pltpu.VMEM((2, CHUNKS, 4, CHUNK, FEATURES), BF16),
            pltpu.VMEM((2, CHUNKS, 4, CHUNK, FEATURES), BF16),
            pltpu.SemaphoreType.DMA((7,)),
            pltpu.SemaphoreType.DMA((2, len(PIECES), 4)),
            pltpu.SemaphoreType.DMA((2, len(PIECES), 4)),
            pltpu.SemaphoreType.DMA((CHUNKS, 2, 2, 3)),
            pltpu.SemaphoreType.DMA((CHUNKS, 2, 2, 3)),
            pltpu.SemaphoreType.DMA((CHUNKS, 2, 4)),
            pltpu.SemaphoreType.DMA((CHUNKS, 2, 4)),
            pltpu.SemaphoreType.DMA((2, CHUNKS, 4)),
            pltpu.SemaphoreType.DMA((2, CHUNKS, 4)),
            pltpu.SemaphoreType.DMA((4,)),
            pltpu.SemaphoreType.DMA((CHUNKS,)),
        ],
        compiler_params=pltpu.CompilerParams(
            collective_id=0, has_side_effects=True, vmem_limit_bytes=56 * 1024 * 1024
        ),
    )(
        routed_x,
        norm_gain.reshape(NZ, 1, FEATURES),
        w_query,
        w_key,
        w_value,
        w_out,
        counts,
        router_weight.reshape(CHUNKS, CHUNK),
    )


def solution(mesh):
    return jax.shard_map(
        body,
        mesh=mesh,
        in_specs=(
            P("ctx", "tp"),
            P(),
            P(None, "tp"),
            P(None, "tp"),
            P(None, "tp"),
            P("tp", None),
            P("ctx"),
            P("ctx"),
            P("ctx"),
        ),
        out_specs=P("ctx", "tp"),
        check_vma=False,
    )
```

time: 131 us -> 108 us (0.82)
  the two profiles are of different devices: /device:TPU:22 before, /device:TPU:4 now
where the time goes in v2:
time: 108 us; the launch traced here: 107 us
  Pallas kernels  104 us (96%)
  local copies, waits for them, and re-layouts  1.77 us (2%)
    pallas_call x1, Pallas kernels, body(): pl.pallas_call(kernel, out_shape=jax.ShapeDtypeStruct((ROWS, FEATURES), B...  104 us

profile of v2, /device:TPU:4, one launch (start us, length us, event | category | flops | bytes accessed | tf_op | source)
XLA Modules:
  0.0 106.5 jit_solution(10294563093153216007)
XLA Ops:
  0.7 104.1 %shard_map.82 = bf16[384,512]{1,0:T(8,128)(2,1)} custom-call(bf16[384,512]{1,0:T(8,128)(2,1)} %x_hbm.1, f32[8,1,512]{2,1,0:T(1,128)} %bitcast.2, bf16[4096,512]{1,0:T(8,128)(2,1)} %wq_hbm.1, bf16[4096,128]{1,0:T(8,128)(2,1)} %wk_hbm.1, bf16[4096,128]{1,0:T(8,128)(2,1)} %wv_hbm.1, bf16[512,4096]{1,0:T(8,128)(2,1)} %wo_hbm.1, s32[1]{0:T(128)S(6)} %copy.10.count_ref, ...), custom_call_target="tpu_custom_call" | custom-call | tf_op jit(solution)/shard_map/pallas_call | solution.py:373
  104.8 1.8 %copy.11 = bf16[384,512]{1,0:T(8,128)(2,1)} copy(bf16[384,512]{1,0:T(8,128)(2,1)} %shard_map.82) | data formatting | bytes 786432

commit v3 on v2

--- a/solution.py
+++ b/solution.py
@@ -25,9 +25,9 @@
 SCHEDULE = (
     "zs0 zs1 zs2 own", "z01 pj01 z11 z21", "pj11 z02 pj02 z12", "z22 pj12 z03 pj03",
     "z13 zs3 z23 pj13", "zs4 zs5 zs6 z04", "pj04 fin0 kva0 fq0", "z14 z31 z24 pj14",
-    "fin1 kva1 fq1 z41", "z51 z61 pj21 z32", "z42 kvb0 z52 z62", "pj22 z33 kvb1 z43",
+    "fin1 kva1 fq1 z41", "z51 z61 pj21 kvb0", "z32 z42 z52 z62", "pj22 z33 kvb1 z43",
     "z53 z63 pj23 z34", "z44 z54 z64 pk24", "fin2 kva2 pq24 fq2", "gq kvc0 kvd0 at00",
-    "kvb2 kvc1 gw al1", "kvd1 ap1 kvc2 al2", "kvd2 at32 gs at02", "ho0 rs01 tma0 at12",
+    "kvb2 kvc1 gw al0", "kvd1 ap1 kvc2 al1", "kvd2 at02 ho0 rs01", "tma0 at32 gs at12",
     "rs02 ho1 rs11 tma1", "tmb0 at22 gr ho2", "rs21 tma2 rs12 rs03", "tmb1 rs22 rs13 rs04",
     "tmb2 rs23 rs14 rs05", "rs24 rs15 rs25",
 )
@@ -248,18 +248,22 @@
         groups = jnp.where(guest, jnp.where(host, NX, 0), jnp.where(lent, 0, x + 1))
         chunk = jnp.minimum(jnp.int32(r), 2)
 
-        @pl.loop(0, groups)
+        pairs = lax.div(groups, 2)
+
+        @pl.loop(0, pairs)
+        def _(i):
+            absorb(r, chunk, jnp.int32(j), 2 * i, last)
+            absorb(r, chunk, jnp.int32(j), 2 * i + 1, last)
+
+        @pl.loop(2 * pairs, groups)
         def _(g):
             absorb(r, chunk, jnp.int32(j), g, last)
 
     def attend_pair(j):
         pl.loop(0, x + 1)(lambda g: absorb(0, 0, jnp.int32(j), g, x, pair=True))
 
-    def attend_many(first):
-        if first == 1:
-            pl.loop(1, 4)(lambda r: attend(r, 0))
-        else:
-            pl.loop(2, 4)(lambda r: attend(r, 1))
+    def attend_many(j):
+        pl.loop(1 + j, 4)(lambda r: attend(r, j))
 
     def guest_copy(back):
         i = 1 if back else 0

time: 108 us -> 106 us (0.981)
  no operation moved by 1% of the time
where the time goes in v3:
time: 106 us; the launch traced here: 105 us
  Pallas kernels  103 us (97%)
  local copies, waits for them, and re-layouts  1.77 us (2%)
    pallas_call x1, Pallas kernels, body(): pl.pallas_call(kernel, out_shape=jax.ShapeDtypeStruct((ROWS, FEATURES), B...  103 us

profile of v3, /device:TPU:4, one launch (start us, length us, event | category | flops | bytes accessed | tf_op | source)
XLA Modules:
  0.0 105.5 jit_solution(11681228185139718588)
XLA Ops:
  0.7 103.1 %shard_map.82 = bf16[384,512]{1,0:T(8,128)(2,1)} custom-call(bf16[384,512]{1,0:T(8,128)(2,1)} %x_hbm.1, f32[8,1,512]{2,1,0:T(1,128)} %bitcast.2, bf16[4096,512]{1,0:T(8,128)(2,1)} %wq_hbm.1, bf16[4096,128]{1,0:T(8,128)(2,1)} %wk_hbm.1, bf16[4096,128]{1,0:T(8,128)(2,1)} %wv_hbm.1, bf16[512,4096]{1,0:T(8,128)(2,1)} %wo_hbm.1, s32[1]{0:T(128)S(6)} %copy.10.count_ref, ...), custom_call_target="tpu_custom_call" | custom-call | tf_op jit(solution)/shard_map/pallas_call | solution.py:377
  103.7 1.8 %copy.11 = bf16[384,512]{1,0:T(8,128)(2,1)} copy(bf16[384,512]{1,0:T(8,128)(2,1)} %shard_map.82) | data formatting | bytes 786432

commit v4 on v3

--- a/solution.py
+++ b/solution.py
@@ -20,16 +20,16 @@
 BF16 = jnp.bfloat16
 F32 = jnp.float32
 
-PIECES = ((0, 128, 0), (128, 64, 1), (192, 64, 1))
+PIECES = ((0, 64, 0), (64, 64, 0), (128, 64, 1), (192, 64, 1))
 PIECES += ((256, 32, 2), (288, 32, 2), (320, 32, 2), (352, 32, 2))
 SCHEDULE = (
-    "zs0 zs1 zs2 own", "z01 pj01 z11 z21", "pj11 z02 pj02 z12", "z22 pj12 z03 pj03",
-    "z13 zs3 z23 pj13", "zs4 zs5 zs6 z04", "pj04 fin0 kva0 fq0", "z14 z31 z24 pj14",
-    "fin1 kva1 fq1 z41", "z51 z61 pj21 kvb0", "z32 z42 z52 z62", "pj22 z33 kvb1 z43",
-    "z53 z63 pj23 z34", "z44 z54 z64 pk24", "fin2 kva2 pq24 fq2", "gq kvc0 kvd0 at00",
-    "kvb2 kvc1 gw al0", "kvd1 ap1 kvc2 al1", "kvd2 at02 ho0 rs01", "tma0 at32 gs at12",
-    "rs02 ho1 rs11 tma1", "tmb0 at22 gr ho2", "rs21 tma2 rs12 rs03", "tmb1 rs22 rs13 rs04",
-    "tmb2 rs23 rs14 rs05", "rs24 rs15 rs25",
+    "zs0 zs1 zs3 own", "z01 z11 pj01 zs2", "z02 z12 pj02 z31", "z21 pj11 z13 z03",
+    "pj03 z32 zs4 zs6", "zs7 z14 zs5 z04", "pj04 fin0 kva0 fq0", "z22 pj12 z33 z41",
+    "z71 z61 z23 pj13", "z51 pj21 z34 kvb0", "z72 z62 z42 z24", "pj14 fin1 kva1 fq1",
+    "z52 pj22 z73 z63", "z43 z53 pj23 kvb1", "kvc0 z74 z44 z64", "z54 pk24 fin2 kva2",
+    "pq24 fq2 gq kvd0", "at00 kvb2 kvc1 gw", "al0 kvd1 at01 kvc2", "al1 kvd2 at02 ho0",
+    "rs01 tma0 at32 gs", "at12 rs02 ho1 rs11", "tma1 tmb0 at22 gr", "ho2 rs21 tma2 rs12",
+    "rs03 tmb1 rs22 rs13", "rs04 tmb2 rs23 rs14", "rs05 rs24 rs15 rs25",
 )
 
 
@@ -259,11 +259,8 @@
         def _(g):
             absorb(r, chunk, jnp.int32(j), g, last)
 
-    def attend_pair(j):
-        pl.loop(0, x + 1)(lambda g: absorb(0, 0, jnp.int32(j), g, x, pair=True))
-
     def attend_many(j):
-        pl.loop(1 + j, 4)(lambda r: attend(r, j))
+        pl.loop(1, 4)(lambda r: attend(r, j))
 
     def guest_copy(back):
         i = 1 if back else 0
@@ -359,7 +356,7 @@
     steps |= {"pq": lambda k, h: z_project(k, h, keys=False), "fq": finish_queries}
     steps |= {"kva": kva, "kvb": kvb, "kvc": kvc, "kvd": kvd}
     steps |= {"gq": guest_query, "gw": guest_wait, "gs": guest_send, "gr": guest_return}
-    steps |= {"al": attend_many, "ap": attend_pair, "own": own, "at": attend, "ho": heads, "tma": lambda r: terms(r, (3, -3)), "tmb": lambda r: terms(r, (2, -2, 1, -1, 0)), "rs": rs}
+    steps |= {"al": attend_many, "own": own, "at": attend, "ho": heads, "tma": lambda r: terms(r, (3, -3)), "tmb": lambda r: terms(r, (2, -2, 1, -1, 0)), "rs": rs}
     for event in " ".join(SCHEDULE).split():
         name = event.rstrip("0123456789")
         steps[name](*map(int, event[len(name) :]))

time: 106 us -> 106 us (level)
  no operation moved by 1% of the time
where the time goes in v4:
time: 106 us; the launch traced here: 105 us
  Pallas kernels  103 us (97%)
  local copies, waits for them, and re-layouts  1.77 us (2%)
    pallas_call x1, Pallas kernels, body(): pl.pallas_call(kernel, out_shape=jax.ShapeDtypeStruct((ROWS, FEATURES), B...  103 us

profile of v4, /device:TPU:4, one launch (start us, length us, event | category | flops | bytes accessed | tf_op | source)
XLA Modules:
  0.0 105.4 jit_solution(6535186085821084116)
XLA Ops:
  0.7 103.0 %shard_map.82 = bf16[384,512]{1,0:T(8,128)(2,1)} custom-call(bf16[384,512]{1,0:T(8,128)(2,1)} %x_hbm.1, f32[8,1,512]{2,1,0:T(1,128)} %bitcast.2, bf16[4096,512]{1,0:T(8,128)(2,1)} %wq_hbm.1, bf16[4096,128]{1,0:T(8,128)(2,1)} %wk_hbm.1, bf16[4096,128]{1,0:T(8,128)(2,1)} %wv_hbm.1, bf16[512,4096]{1,0:T(8,128)(2,1)} %wo_hbm.1, s32[1]{0:T(128)S(6)} %copy.10.count_ref, ...), custom_call_target="tpu_custom_call" | custom-call | tf_op jit(solution)/shard_map/pallas_call | solution.py:374
  103.6 1.8 %copy.11 = bf16[384,512]{1,0:T(8,128)(2,1)} copy(bf16[384,512]{1,0:T(8,128)(2,1)} %shard_map.82) | data formatting | bytes 786432
